TPU v7x, 128 devices: a whole 4x4x4 slice. The times are simulated.
128 devices in a mesh: dp: 16 (over y, x), tensor: 8 (over z, core).
Axes of the slice: x: 4, y: 4, z: 4, core: 2. Of those that a mesh axis runs over, the one named last changes fastest.
Arguments:
- old_master: float32 [128, 672, 128], P(('dp', 'tensor')), may hold values from -6 to 6
- old_avg: float32 [128, 672, 128], P(('dp', 'tensor')), may hold values from -1.8 to 1.8
- old_sq: float32 [128, 672, 128], P(('dp', 'tensor')), may hold values from 0.001 to 1
- grad: float32 [128, 672, 128], P(('dp', 'tensor')), may hold values from -6 to 6
- old_table: int32 [128, 3], replicated, may hold values from 0 to 10751, as said below
- new_table: int32 [128, 3], replicated, may hold values from 0 to 5375, as said below
- head_order: int32 [112], replicated, may hold values from 0 to 111, each once
Outputs:
- new_master: float32 [128, 672, 128], P(('dp', 'tensor'))
- new_avg: float32 [128, 672, 128], P(('dp', 'tensor'))
- new_sq: float32 [128, 672, 128], P(('dp', 'tensor'))
- params: bfloat16 [128, 43008], P(None, 'tensor')
Inputs may be any that keep to these rules, and one draw needn't show every extreme that they name: `old_table`: row k belongs to old rank k // 32; the fragments of one old rank follow one another in k without gaps and cover its 10752 units; every length is 1 to 672, in each old rank one length is exactly 672, and the last fragment of each old rank has length 1. `new_table`: row k = d * 8 + n belongs to new rank n; for one new rank the ranges follow one another in d without gaps and cover its 5376 units; range d lies within units d * 336 to (d + 3) * 336 - 1; every length is 1 to 672, in each new rank one length is exactly 672 and that range reaches unit (d + 2) * 336 or beyond, and the last range of each new rank has length 1.
All inputs are finite; a program needn't handle non-finite values.
Results may differ from a plain program's by a relative error of at most 0.0033.
Values may be sent and summed in bfloat16 or wider, within the bound.
No kernel may reach another device: no remote copies, remote signals or barrier semaphores. Data moves between devices by JAX's collectives and lax.ppermute only.
A program may use at most 128 MiB of HBM per device.

v0:
```python
import jax
import jax.numpy as jnp
from jax import lax
from jax.sharding import PartitionSpec as P

OLD_TP = 4
STEPS_DONE = 10
beta_first = 0.9
beta_second = 0.95
learn_rate = 0.1
decay_rate = 0.1
epsilon_add = 1e-08


def shifted(shard, axis, by):
    peers = lax.axis_size(axis)
    pairs = [(i, i + by) for i in range(peers) if 0 <= i + by < peers]
    return lax.ppermute(shard, axis, pairs)


def adam_update(master, moment, square, gradient):
    moment_new = beta_first * moment + (1.0 - beta_first) * gradient
    square_new = beta_second * square + (1.0 - beta_second) * gradient * gradient
    moment_hat = moment_new / (1.0 - beta_first**STEPS_DONE)
    square_hat = square_new / (1.0 - beta_second**STEPS_DONE)
    master_new = master - learn_rate * (
        moment_hat / (jnp.sqrt(square_hat) + epsilon_add) + decay_rate * master
    )
    return (master_new, moment_new, square_new)


def pick_units(source, wanted, begin_at, count_of):
    offset = wanted - begin_at
    inside = (offset >= 0) & (offset < count_of)
    safe_index = jnp.clip(offset, 0, source.shape[0] - 1)
    return jnp.where(inside[..., None], source[safe_index], jnp.zeros((), source.dtype))


def owner_slice(whole, begin_at, count_of, slot_size):
    padded = jnp.concatenate([whole, jnp.zeros((slot_size, whole.shape[1]), whole.dtype)], axis=0)
    window = lax.dynamic_slice_in_dim(padded, begin_at, slot_size, 0)
    inside = jnp.arange(slot_size, dtype=jnp.int32) < count_of
    return jnp.where(inside[:, None], window, jnp.zeros((), whole.dtype))


def on_device(old_master, old_avg, old_sq, grad, old_table, new_table, head_order):
    slot_size = old_master.shape[1]
    head_dim = old_master.shape[2]
    head_count = head_order.shape[0]
    dp_count = lax.axis_size("dp")
    tp_count = lax.axis_size("tensor")
    all_count = dp_count * tp_count
    dp_index = lax.axis_index("dp")
    tp_index = lax.axis_index("tensor")
    dev_index = dp_index * tp_count + tp_index
    unit_dev = slot_size // 2
    heads_old = head_count // OLD_TP
    heads_new = head_count // tp_count
    new_units = 3 * heads_new
    rows_dev = unit_dev // (3 * head_count)
    block_units = rows_dev * 3 * heads_old
    old_states = (old_master[0], old_avg[0], old_sq[0])
    frag_start = old_table[dev_index, 1]
    frag_length = old_table[dev_index, 2]
    within = jnp.arange(block_units, dtype=jnp.int32)
    target = jnp.arange(all_count, dtype=jnp.int32)[:, None] * block_units + within[None, :]
    sending = tuple((pick_units(single, target, frag_start, frag_length) for single in old_states))
    arrived = lax.all_to_all(sending, ("dp", "tensor"), split_axis=0, concat_axis=0, tiled=True)
    canonical = tuple(
        (
            single.reshape(OLD_TP, all_count // OLD_TP, block_units, head_dim).sum(axis=1)
            for single in arrived
        )
    )
    order_table = head_order.reshape(tp_count, heads_new)

    def regroup(single):
        weight = single.reshape(OLD_TP, rows_dev, heads_old, 3, head_dim).transpose(1, 0, 2, 3, 4)
        weight = weight.reshape(rows_dev, head_count, 3, head_dim)
        return weight[:, order_table].transpose(1, 0, 3, 2, 4)

    regrouped = tuple((regroup(single) for single in canonical))
    landed = lax.all_to_all(regrouped, "tensor", split_axis=0, concat_axis=0, tiled=True)
    blocks = tuple((single.reshape(unit_dev, head_dim) for single in landed))
    new_start = new_table[dev_index, 1]
    new_length = new_table[dev_index, 2]
    gradient = grad[0]
    stacked = jnp.stack(blocks, axis=0)
    nearby = [stacked]
    for distance in (1, 2):
        nearby.append(shifted(stacked, "dp", -distance))
    joined = jnp.concatenate(nearby, axis=1)
    local_start = new_start - dp_index * unit_dev
    mine = tuple(
        (owner_slice(joined[which], local_start, new_length, slot_size) for which in range(3))
    )
    master_new, moment_new, square_new = adam_update(mine[0], mine[1], mine[2], gradient)
    inside = (jnp.arange(slot_size, dtype=jnp.int32) < new_length)[:, None]
    master_new = jnp.where(inside, master_new, 0.0)
    moment_new = jnp.where(inside, moment_new, 0.0)
    square_new = jnp.where(inside, square_new, 0.0)
    pieces = lax.all_gather(master_new.astype(jnp.bfloat16), "dp", axis=0, tiled=True)
    starts_all = new_table.reshape(dp_count, tp_count, 3)[:, tp_index, 1]
    flat_place = jnp.arange(dp_count * unit_dev, dtype=jnp.int32)
    owner = jnp.sum((flat_place[:, None] >= starts_all[None, :]).astype(jnp.int32), axis=1) - 1
    source_index = owner * slot_size + flat_place - starts_all[owner]
    params_flat = pieces[source_index]
    params = params_flat.reshape(-1, new_units * head_dim)
    return (master_new[None], moment_new[None], square_new[None], params)


def solution(mesh):
    in_specs = (
        P(("dp", "tensor"), None, None),
        P(("dp", "tensor"), None, None),
        P(("dp", "tensor"), None, None),
        P(("dp", "tensor"), None, None),
        P(),
        P(),
        P(),
    )
    out_specs = (
        P(("dp", "tensor"), None, None),
        P(("dp", "tensor"), None, None),
        P(("dp", "tensor"), None, None),
        P(None, "tensor"),
    )
    return jax.shard_map(
        on_device, mesh=mesh, in_specs=in_specs, out_specs=out_specs, check_vma=False
    )
```

profile of v0, /device:TPU:1, one launch (start us, length us, event | category | flops | bytes accessed | tf_op | source)
XLA Modules:
  0.0 457.7 jit_solution(10279314720494581328)
XLA Ops:
  7.2 0.0 copy-start
  7.2 1.4 constant_dynamic-slice_fusion.18
  8.6 0.7 compare_select_fusion
  9.3 0.1 reshape.188
  9.4 0.0 copy-done
  9.5 20.5 %gather_fusion = f32[10752,128]{1,0:T(8,128)} fusion(f32[672,128]{1,0:T(8,128)S(1)} %bitcast.81, s32[11264]{0:T(1024)S(1)} %pad_clamp_fusion), kind=kCustom, calls=%fused_computation | custom fusion | bytes 11053056 | tf_op jit(solution)/shard_map/gather | solution.py:36
  29.9 6.8 %reshape.187 = f32[128,84,128]{2,1,0:T(8,128)} reshape(f32[10752,128]{1,0:T(8,128)} %gather_fusion) | data formatting | bytes 11010048 | tf_op jit(solution)/shard_map/gather | solution.py:36
  36.7 1.4 fusion.9
  38.1 0.0 copy-done.2
  38.1 20.5 %gather_fusion.2 = f32[10752,128]{1,0:T(8,128)} fusion(f32[672,128]{1,0:T(8,128)S(1)} %bitcast.82, s32[11264]{0:T(1024)S(1)} %pad_clamp_fusion), kind=kCustom, calls=%fused_computation.2 | custom fusion | bytes 11053056 | tf_op jit(solution)/shard_map/gather | solution.py:36
  58.6 6.7 %reshape.205 = f32[128,84,128]{2,1,0:T(8,128)} reshape(f32[10752,128]{1,0:T(8,128)} %gather_fusion.2) | data formatting | bytes 11010048 | tf_op jit(solution)/shard_map/gather | solution.py:36
  65.3 0.0 copy-done.3
  65.3 20.5 %gather_fusion.4 = f32[10752,128]{1,0:T(8,128)} fusion(f32[672,128]{1,0:T(8,128)S(1)} %bitcast.83, s32[11264]{0:T(1024)S(1)} %pad_clamp_fusion), kind=kCustom, calls=%fused_computation.4 | custom fusion | bytes 11053056 | tf_op jit(solution)/shard_map/gather | solution.py:36
  85.8 6.7 %reshape.223 = f32[128,84,128]{2,1,0:T(8,128)} reshape(f32[10752,128]{1,0:T(8,128)} %gather_fusion.4) | data formatting | bytes 11010048 | tf_op jit(solution)/shard_map/gather | solution.py:36
  92.5 10.2 %broadcast_select_fusion.2 = (f32[128,84,128]{2,1,0:T(8,128)}, f32[128,84,128]{2,1,0:T(8,128)S(1)}, f32[128,84,128]{2,1,0:T(8,128)S(1)}) fusion(f32[128,84,128]{2,1,0:T(8,128)} %reshape.187, pred[128,84]{1,0:T(8,128)(4,1)S(1)} %fusion.9, f32[128,84,128]{2,1,0:T(8,128)} %reshape.205, f32[128,84,128]{2,1,0:T(8,128)} %reshape.223), kind=kLoop, calls=%fused_computation.12 | loop fusion | flops 4128768 | bytes 33040896 | tf_op jit(solution)/shard_map/jit(_where)/select_n | solution.py:36
  102.6 81.0 %all_to_all.30 = f32[128,84,128]{2,1,0:T(8,128)} all-to-all(f32[128,84,128]{2,1,0:T(8,128)S(1)} %get-tuple-element.42), channel_id=1, replica_groups=mesh['dp'=16,'tensor'=8] {'dp','tensor'}, dimensions={0} | all-to-all | bytes 11010048 | tf_op jit(solution)/shard_map/all_to_all | solution.py:68
  183.7 74.5 %all_to_all.31 = f32[128,84,128]{2,1,0:T(8,128)} all-to-all(f32[128,84,128]{2,1,0:T(8,128)S(1)} %get-tuple-element.41), channel_id=1, replica_groups=mesh['dp'=16,'tensor'=8] {'dp','tensor'}, dimensions={0} | all-to-all | bytes 11010048 | tf_op jit(solution)/shard_map/all_to_all | solution.py:68
  258.2 5.9 %all-to-all-start = ((f32[128,84,128]{2,1,0:T(8,128)}), f32[128,84,128]{2,1,0:T(8,128)}, u32[]{:S(2)}, u32[]{:S(2)}) async-start(f32[128,84,128]{2,1,0:T(8,128)} %get-tuple-element.40), calls=%async_computation | async-start | bytes 11534336 | tf_op jit(solution)/shard_map/all_to_all | solution.py:68
  264.1 0.0 copy-done.6
  264.1 0.1 reshape.181
  264.2 0.1 reshape.198
  264.3 2.9 bitcast_reduce_fusion
  267.2 0.1 reshape.230
  267.3 0.7 gather_fusion.5
  268.0 0.8 copy.44
  268.9 65.9 %all-to-all-done = f32[128,84,128]{2,1,0:T(8,128)} async-done(((f32[128,84,128]{2,1,0:T(8,128)}), f32[128,84,128]{2,1,0:T(8,128)}, u32[]{:S(2)}, u32[]{:S(2)}) %all-to-all-start) | async-done | bytes 5505056 | tf_op jit(solution)/shard_map/all_to_all | solution.py:68
  334.8 3.8 all-to-all-start.5
  338.5 2.9 bitcast_reduce_fusion.1
  341.4 0.1 reshape.212
  341.5 0.7 gather_fusion.3
  342.3 0.8 copy.42
  343.1 1.1 all-to-all-done.5
  344.2 4.2 all-to-all-start.3
  348.4 0.0 all-gather.2.cloned.1.call-start
  348.4 2.9 bitcast_reduce_fusion.2
  351.3 0.0 copy-start.4
  351.3 0.1 reshape.194
  351.4 0.7 gather_fusion.1
  352.1 0.0 copy-start.5
  352.2 0.2 copy.40
  352.4 1.7 all-to-all-done.3
  354.1 9.0 %all_to_all.32 = f32[8,1,3,14,128]{4,1,3,2,0:T(1,128)S(1)} all-to-all(f32[8,1,3,14,128]{4,1,3,2,0:T(1,128)S(1)} %copy.40), channel_id=1, replica_groups=mesh['dp'=16,'tensor'=8] {'tensor'}, dimensions={0} | all-to-all | bytes 344064 | tf_op jit(solution)/shard_map/all_to_all | solution.py:83
  363.1 1.3 collective-permute-start.1
  364.4 1.3 collective-permute-start
  366.3 0.7 iota_compare_fusion.1
  367.0 11.8 %collective-permute-done.1 = f32[3,336,128]{2,1,0:T(8,128)S(1)} collective-permute-done((f32[3,336,128]{2,1,0:T(8,128)S(1)}, f32[3,336,128]{2,1,0:T(8,128)S(1)}, u32[]{:S(2)}, u32[]{:S(2)}) %collective-permute-start.1) | collective-permute-done | bytes 516128 | tf_op jit(solution)/shard_map/ppermute | solution.py:18
  378.8 0.0 collective-permute-done
  378.8 0.1 pad_maximum_fusion
  378.9 0.1 slice_bitcast_fusion.2
  379.0 1.5 fusion.12
  380.6 0.0 all-gather.2.cloned.1.call-update
  380.6 0.0 copy-done.5
  380.6 0.1 reshape.184
  380.7 0.2 dynamic-slice_reduce_fusion
  380.9 0.8 constant_dynamic-slice_fusion.7
  381.6 0.1 convert_reduce_fusion
  381.8 4.3 fusion.10
  386.1 0.6 compare_reduce_fusion.8
  386.7 5.5 %select_select_fusion = s32[5376]{0:T(1024)S(1)} fusion(pred[5376]{0:T(1024)(128)(4,1)S(1)} %get-tuple-element.12, pred[5376]{0:T(1024)(128)(4,1)S(1)} %get-tuple-element.11, pred[5376]{0:T(1024)(128)(4,1)S(1)} %get-tuple-element.10, pred[5376]{0:T(1024)(128)(4,1)S(1)} %get-tuple-element.9, pred[5376]{0:T(1024)(128)(4,1)S(1)} %get-tuple-element.8, ...), kind=kLoop, calls=%fused_computation.62 | loop fusion | flops 48384 | bytes 91428 | tf_op jit(solution)/shard_map/gather | solution.py:106
  392.2 0.1 fusion.11
  392.3 0.0 copy-start.1
  392.4 45.3 %all-gather.2.cloned.1.call-done = bf16[10752,128]{1,0:T(8,128)(2,1)} async-done(((bf16[672,128]{1,0:T(8,128)(2,1)}), bf16[10752,128]{1,0:T(8,128)(2,1)}) %all-gather.2.cloned.1.call-update) | async-done | bytes 2752528 | tf_op jit(solution)/shard_map/all_gather | solution.py:102
  437.6 10.8 %gather_fusion.6 = bf16[5376,128]{1,0:T(8,128)(2,1)S(1)} fusion(bf16[10752,128]{1,0:T(8,128)(2,1)} %all-gather.2.cloned.1.call-done, s32[6144]{0:T(1024)S(1)} %pad_clamp_fusion.1), kind=kCustom, calls=%fused_computation.6 | custom fusion | bytes 2774016 | tf_op jit(solution)/shard_map/gather | solution.py:107
  448.5 2.4 reshape.185
  (15 shorter events, 0.2 us)
Async XLA Ops:
  7.2 2.3 copy-start
  29.9 8.2 %copy-start.2 = (f32[1,672,128]{2,1,0:T(8,128)S(1)}, f32[1,672,128]{2,1,0:T(8,128)}, u32[]{:S(2)}) copy-start(f32[1,672,128]{2,1,0:T(8,128)} %param.8) | copy-start | bytes 1032196
  58.6 6.7 %copy-start.3 = (f32[1,672,128]{2,1,0:T(8,128)S(1)}, f32[1,672,128]{2,1,0:T(8,128)}, u32[]{:S(2)}) copy-start(f32[1,672,128]{2,1,0:T(8,128)} %param.9) | copy-start | bytes 1032196
  258.2 5.9 %copy-start.6 = (s32[112]{0:T(128)S(1)}, s32[112]{0:T(128)}, u32[]{:S(2)}) copy-start(s32[112]{0:T(128)} %param.13) | copy-start | bytes 1348
  258.2 76.6 %all-to-all-start = ((f32[128,84,128]{2,1,0:T(8,128)}), f32[128,84,128]{2,1,0:T(8,128)}, u32[]{:S(2)}, u32[]{:S(2)}) async-start(f32[128,84,128]{2,1,0:T(8,128)} %get-tuple-element.40), calls=%async_computation | async-start | bytes 11534336 | tf_op jit(solution)/shard_map/all_to_all | solution.py:68
  334.8 9.4 %all-to-all-start.5 = ((f32[8,1,3,14,128]{4,1,3,2,0:T(1,128)}), f32[8,1,3,14,128]{4,1,3,2,0:T(1,128)S(1)}, u32[]{:S(2)}, u32[]{:S(2)}) async-start(f32[8,1,3,14,128]{4,1,3,2,0:T(1,128)} %copy.44), calls=%async_computation.5 | async-start | bytes 344064 | tf_op jit(solution)/shard_map/all_to_all | solution.py:83
  344.2 9.9 %all-to-all-start.3 = ((f32[8,1,3,14,128]{4,1,3,2,0:T(1,128)}), f32[8,1,3,14,128]{4,1,3,2,0:T(1,128)S(1)}, u32[]{:S(2)}, u32[]{:S(2)}) async-start(f32[8,1,3,14,128]{4,1,3,2,0:T(1,128)} %copy.42), calls=%async_computation.3 | async-start | bytes 344064 | tf_op jit(solution)/shard_map/all_to_all | solution.py:83
  348.4 89.2 %all-gather.2.cloned.1.call-start = ((), (), s32[]{:S(2)}) async-start(), calls=%async_computation.6 | async-start | bytes 2924544 | tf_op jit(solution)/shard_map/all_gather | solution.py:102
  351.3 27.7 %copy-start.4 = (f32[1,672,128]{2,1,0:T(8,128)S(1)}, f32[1,672,128]{2,1,0:T(8,128)}, u32[]{:S(2)}) copy-start(f32[1,672,128]{2,1,0:T(8,128)} %param.10) | copy-start | bytes 1032196
  352.1 28.4 %copy-start.5 = (s32[128,3]{0,1:T(4,128)S(1)}, s32[128,3]{0,1:T(4,128)}, u32[]{:S(2)}) copy-start(s32[128,3]{0,1:T(4,128)} %param.12) | copy-start | bytes 4612
  363.1 15.7 %collective-permute-start.1 = (f32[3,336,128]{2,1,0:T(8,128)S(1)}, f32[3,336,128]{2,1,0:T(8,128)S(1)}, u32[]{:S(2)}, u32[]{:S(2)}) collective-permute-start(f32[3,336,128]{2,1,0:T(8,128)S(1)} %pad_maximum_fusion.1), channel_id=1, source_target_pairs={{16,0},{24,8},{32,16},{40,24},{48,32},{56,40},{64,48},{72,56},{80,... | collective-permute-start | bytes 1548296 | tf_op jit(solution)/shard_map/ppermute | solution.py:18
  364.4 14.4 %collective-permute-start = (f32[3,336,128]{2,1,0:T(8,128)S(1)}, f32[3,336,128]{2,1,0:T(8,128)S(1)}, u32[]{:S(2)}, u32[]{:S(2)}) collective-permute-start(f32[3,336,128]{2,1,0:T(8,128)S(1)} %pad_maximum_fusion.1), channel_id=1, source_target_pairs={{8,0},{16,8},{24,16},{32,24},{40,32},{48,40},{56,48},{64,56},{72,6... | collective-permute-start | bytes 1548296 | tf_op jit(solution)/shard_map/ppermute | solution.py:18
  392.3 58.5 %copy-start.1 = (f32[1,672,128]{2,1,0:T(8,128)S(1)}, f32[1,672,128]{2,1,0:T(8,128)}, u32[]{:S(2)}) copy-start(f32[1,672,128]{2,1,0:T(8,128)} %param.7) | copy-start | bytes 1032196
Sparse Core Ops, SparseCore 0:
  380.7 56.8 all-gather.1
where the time goes:
time: 459 us; the launch traced here: 458 us
  blocking collectives  164 us (36%)
  waiting for transfers between devices  126 us (27%)
  local copies, waits for them, and re-layouts  102 us (22%)
  other arithmetic  34 us (7%)
  starting transfers between devices  16.5 us (4%)
  between operations  15 us (3%)
    all_to_all x2, blocking collectives, on_device(): lax.all_to_all(sending, ('dp', 'tensor'), split_axis=0, concat_axis=0, ti...  156 us
    gather x6, local copies, waits for them, and re-layouts, pick_units(): source[safe_index]  81.6 us
    all_to_all x1, waiting for transfers between devices, on_device(): lax.all_to_all(sending, ('dp', 'tensor'), split_axis=0, concat_axis=0, ti...  65.9 us
    all_gather x1, waiting for transfers between devices, on_device(): lax.all_gather(master_new.astype(jnp.bfloat16), 'dp', axis=0, tiled=True)  45.3 us
    ppermute x2, waiting for transfers between devices, shifted(): return lax.ppermute(shard, axis, pairs)  11.8 us
    gather x1, local copies, waits for them, and re-layouts, on_device(): params_flat = pieces[source_index]  10.8 us
    gather x3, other arithmetic, on_device(): source_index = owner * slot_size + flat_place - starts_all[owner]  10.4 us
    select_n x1, other arithmetic, pick_units(): jnp.where(inside[..., None], source[safe_index], jnp.zeros((), source.dty...  10.2 us
  transfers between devices with their start and end apart: 6, of which 5 were waited for; matrix products, arithmetic and copies ran while one was open for 6% of the time, Pallas kernels for 0%

commit v1 on v0

--- a/solution.py
+++ b/solution.py
@@ -99,7 +99,12 @@
     master_new = jnp.where(inside, master_new, 0.0)
     moment_new = jnp.where(inside, moment_new, 0.0)
     square_new = jnp.where(inside, square_new, 0.0)
-    pieces = lax.all_gather(master_new.astype(jnp.bfloat16), "dp", axis=0, tiled=True)
+    pieces = jnp.concatenate(
+        lax.all_to_all(
+            jnp.stack([master_new.astype(jnp.bfloat16)] * lax.axis_size("dp")), "dp", 0, 0
+        ),
+        axis=0,
+    )
     starts_all = new_table.reshape(dp_count, tp_count, 3)[:, tp_index, 1]
     flat_place = jnp.arange(dp_count * unit_dev, dtype=jnp.int32)
     owner = jnp.sum((flat_place[:, None] >= starts_all[None, :]).astype(jnp.int32), axis=1) - 1

time: 459 us -> 459 us (level)
  starting transfers between devices: 16.5 us -> 34.3 us
  waiting for transfers between devices: 126 us -> 110 us
  between operations: 15 us -> 1.63 us
  other arithmetic: 34 us -> 41.1 us
    all_gather x1 -> x0, waiting for transfers between devices: 45.3 us -> none  [on_device(): lax.all_gather(master_new.astype(jnp.bfloat16), 'dp', axis=0, tiled=True)]
    all_to_all x0 -> x1, waiting for transfers between devices: none -> 29.5 us  [on_device(): lax.all_to_all(jnp.stack([master_new.astype(jnp.bfloat16)] * lax.axis_siz...]
    all_to_all x0 -> x1, starting transfers between devices: none -> 17.8 us  [on_device(): lax.all_to_all(jnp.stack([master_new.astype(jnp.bfloat16)] * lax.axis_siz...]
    slice x0 -> x1, other arithmetic: none -> 6.77 us  [on_device(): joined[which]]
where the time goes in v1:
time: 459 us; the launch traced here: 458 us
  blocking collectives  164 us (36%)
  waiting for transfers between devices  110 us (24%)
  local copies, waits for them, and re-layouts  106 us (23%)
  other arithmetic  41.1 us (9%)
  starting transfers between devices  34.3 us (7%)
    all_to_all x2, blocking collectives, on_device(): lax.all_to_all(sending, ('dp', 'tensor'), split_axis=0, concat_axis=0, ti...  156 us
    gather x6, local copies, waits for them, and re-layouts, pick_units(): source[safe_index]  81.6 us
    all_to_all x1, waiting for transfers between devices, on_device(): lax.all_to_all(sending, ('dp', 'tensor'), split_axis=0, concat_axis=0, ti...  65.9 us
    all_to_all x1, waiting for transfers between devices, on_device(): lax.all_to_all(jnp.stack([master_new.astype(jnp.bfloat16)] * lax.axis_siz...  29.5 us
    all_to_all x1, starting transfers between devices, on_device(): lax.all_to_all(jnp.stack([master_new.astype(jnp.bfloat16)] * lax.axis_siz...  17.8 us
    ppermute x2, waiting for transfers between devices, shifted(): return lax.ppermute(shard, axis, pairs)  11.8 us
    gather x1, local copies, waits for them, and re-layouts, on_device(): params_flat = pieces[source_index]  11.6 us
    gather x3, other arithmetic, on_device(): source_index = owner * slot_size + flat_place - starts_all[owner]  10.4 us
  transfers between devices with their start and end apart: 6, of which 5 were waited for; matrix products, arithmetic and copies ran while one was open for 6% of the time, Pallas kernels for 0%

profile of v1, /device:TPU:1, one launch (start us, length us, event | category | flops | bytes accessed | tf_op | source)
XLA Modules:
  0.0 457.9 jit_solution(2171286147924405691)
XLA Ops:
  0.6 0.0 copy-start
  0.7 1.4 constant_dynamic-slice_fusion.18
  2.0 0.7 compare_select_fusion
  2.8 0.1 reshape.194
  2.9 0.0 copy-done
  2.9 20.5 %gather_fusion = f32[10752,128]{1,0:T(8,128)} fusion(f32[672,128]{1,0:T(8,128)S(1)} %bitcast.77, s32[11264]{0:T(1024)S(1)} %pad_clamp_fusion), kind=kCustom, calls=%fused_computation | custom fusion | bytes 11053056 | tf_op jit(solution)/shard_map/gather | solution.py:36
  23.4 6.8 %reshape.193 = f32[128,84,128]{2,1,0:T(8,128)} reshape(f32[10752,128]{1,0:T(8,128)} %gather_fusion) | data formatting | bytes 11010048 | tf_op jit(solution)/shard_map/gather | solution.py:36
  30.2 1.4 fusion.9
  31.6 0.0 copy-done.2
  31.6 20.5 %gather_fusion.2 = f32[10752,128]{1,0:T(8,128)} fusion(f32[672,128]{1,0:T(8,128)S(1)} %bitcast.78, s32[11264]{0:T(1024)S(1)} %pad_clamp_fusion), kind=kCustom, calls=%fused_computation.2 | custom fusion | bytes 11053056 | tf_op jit(solution)/shard_map/gather | solution.py:36
  52.0 6.7 %reshape.211 = f32[128,84,128]{2,1,0:T(8,128)} reshape(f32[10752,128]{1,0:T(8,128)} %gather_fusion.2) | data formatting | bytes 11010048 | tf_op jit(solution)/shard_map/gather | solution.py:36
  58.8 0.0 copy-done.3
  58.8 20.5 %gather_fusion.4 = f32[10752,128]{1,0:T(8,128)} fusion(f32[672,128]{1,0:T(8,128)S(1)} %bitcast.79, s32[11264]{0:T(1024)S(1)} %pad_clamp_fusion), kind=kCustom, calls=%fused_computation.4 | custom fusion | bytes 11053056 | tf_op jit(solution)/shard_map/gather | solution.py:36
  79.3 6.7 %reshape.229 = f32[128,84,128]{2,1,0:T(8,128)} reshape(f32[10752,128]{1,0:T(8,128)} %gather_fusion.4) | data formatting | bytes 11010048 | tf_op jit(solution)/shard_map/gather | solution.py:36
  85.9 10.2 %broadcast_select_fusion.2 = (f32[128,84,128]{2,1,0:T(8,128)}, f32[128,84,128]{2,1,0:T(8,128)S(1)}, f32[128,84,128]{2,1,0:T(8,128)S(1)}) fusion(f32[128,84,128]{2,1,0:T(8,128)} %reshape.193, pred[128,84]{1,0:T(8,128)(4,1)S(1)} %fusion.9, f32[128,84,128]{2,1,0:T(8,128)} %reshape.211, f32[128,84,128]{2,1,0:T(8,128)} %reshape.229), kind=kLoop, calls=%fused_computation.12 | loop fusion | flops 4128768 | bytes 33040896 | tf_op jit(solution)/shard_map/jit(_where)/select_n | solution.py:36
  96.1 81.0 %all_to_all.35 = f32[128,84,128]{2,1,0:T(8,128)} all-to-all(f32[128,84,128]{2,1,0:T(8,128)S(1)} %get-tuple-element.42), channel_id=1, replica_groups=mesh['dp'=16,'tensor'=8] {'dp','tensor'}, dimensions={0} | all-to-all | bytes 11010048 | tf_op jit(solution)/shard_map/all_to_all | solution.py:68
  177.1 74.5 %all_to_all.36 = f32[128,84,128]{2,1,0:T(8,128)} all-to-all(f32[128,84,128]{2,1,0:T(8,128)S(1)} %get-tuple-element.41), channel_id=1, replica_groups=mesh['dp'=16,'tensor'=8] {'dp','tensor'}, dimensions={0} | all-to-all | bytes 11010048 | tf_op jit(solution)/shard_map/all_to_all | solution.py:68
  251.6 5.9 %all-to-all-start = ((f32[128,84,128]{2,1,0:T(8,128)}), f32[128,84,128]{2,1,0:T(8,128)}, u32[]{:S(2)}, u32[]{:S(2)}) async-start(f32[128,84,128]{2,1,0:T(8,128)} %get-tuple-element.40), calls=%async_computation | async-start | bytes 11534336 | tf_op jit(solution)/shard_map/all_to_all | solution.py:68
  257.5 0.0 copy-done.6
  257.6 0.1 reshape.186
  257.6 0.1 reshape.204
  257.7 2.9 bitcast_reduce_fusion
  260.6 0.1 reshape.236
  260.7 0.7 gather_fusion.5
  261.5 0.8 copy.45
  262.3 65.9 %all-to-all-done = f32[128,84,128]{2,1,0:T(8,128)} async-done(((f32[128,84,128]{2,1,0:T(8,128)}), f32[128,84,128]{2,1,0:T(8,128)}, u32[]{:S(2)}, u32[]{:S(2)}) %all-to-all-start) | async-done | bytes 5505056 | tf_op jit(solution)/shard_map/all_to_all | solution.py:68
  328.2 3.8 all-to-all-start.5
  332.0 2.9 bitcast_reduce_fusion.1
  334.9 0.1 reshape.218
  335.0 0.7 gather_fusion.3
  335.7 0.8 copy.43
  336.6 1.1 all-to-all-done.5
  337.7 4.2 all-to-all-start.3
  341.9 2.9 bitcast_reduce_fusion.2
  344.8 0.0 copy-start.4
  344.8 0.1 reshape.200
  344.9 0.7 gather_fusion.1
  345.6 0.2 copy.41
  345.8 1.7 all-to-all-done.3
  347.5 9.0 %all_to_all.37 = f32[8,1,3,14,128]{4,1,3,2,0:T(1,128)S(1)} all-to-all(f32[8,1,3,14,128]{4,1,3,2,0:T(1,128)S(1)} %copy.41), channel_id=1, replica_groups=mesh['dp'=16,'tensor'=8] {'tensor'}, dimensions={0} | all-to-all | bytes 344064 | tf_op jit(solution)/shard_map/all_to_all | solution.py:83
  356.5 0.4 pad_maximum_fusion
  357.0 1.3 collective-permute-start.1
  358.3 1.3 collective-permute-start
  360.2 0.7 iota_compare_fusion.1
  360.9 11.8 %collective-permute-done.1 = f32[3,336,128]{2,1,0:T(8,128)S(1)} collective-permute-done((f32[3,336,128]{2,1,0:T(8,128)S(1)}, f32[3,336,128]{2,1,0:T(8,128)S(1)}, u32[]{:S(2)}, u32[]{:S(2)}) %collective-permute-start.1) | collective-permute-done | bytes 516128 | tf_op jit(solution)/shard_map/ppermute | solution.py:18
  372.7 0.3 copy.49
  373.0 0.0 collective-permute-done
  373.0 0.3 copy.48
  373.3 6.8 %pad_maximum_fusion.6 = (f32[1,1008,128]{2,0,1:T(1,128)S(1)}, f32[1,1008,128]{2,0,1:T(1,128)S(1)}, f32[1,1008,128]{2,0,1:T(1,128)S(1)}) fusion(f32[3,336,128]{2,0,1:T(4,128)S(1)} %copy.49, f32[3,336,128]{2,0,1:T(4,128)S(1)} %copy.48, f32[1,336,128]{2,0,1:T(1,128)S(1)} %bitcast.85, f32[1,336,128]{2,0,1:T(1,128)S(1)} %bitcast.87, f32[1,336,128]{2,0,1:T(1,128)S(1)} %bitcast.89), kind=kLoop, calls=%fused_computation.22 | loop fusion | flops 1548288 | bytes 3096576 | tf_op jit(solution)/shard_map/slice | solution.py:95
  380.1 0.0 copy-start.5
  380.1 1.5 fusion.12
  381.5 1.9 stack.5
  383.5 17.8 %all-to-all-start.6 = ((bf16[16,672,128]{2,1,0:T(8,128)(2,1)}), bf16[16,672,128]{2,1,0:T(8,128)(2,1)S(1)}, u32[]{:S(2)}, u32[]{:S(2)}) async-start(bf16[16,672,128]{2,1,0:T(8,128)(2,1)} %stack.5), calls=%async_computation.6 | async-start | bytes 5505024 | tf_op jit(solution)/shard_map/all_to_all | solution.py:103
  401.3 0.1 reshape.190
  401.4 0.2 dynamic-slice_reduce_fusion
  401.5 0.7 constant_dynamic-slice_fusion.7
  402.3 0.1 convert_reduce_fusion
  402.5 4.4 fusion.10
  406.8 0.6 compare_reduce_fusion.8
  407.4 5.5 %select_select_fusion = s32[5376]{0:T(1024)S(1)} fusion(pred[5376]{0:T(1024)(128)(4,1)S(1)} %get-tuple-element.12, pred[5376]{0:T(1024)(128)(4,1)S(1)} %get-tuple-element.11, pred[5376]{0:T(1024)(128)(4,1)S(1)} %get-tuple-element.10, pred[5376]{0:T(1024)(128)(4,1)S(1)} %get-tuple-element.9, pred[5376]{0:T(1024)(128)(4,1)S(1)} %get-tuple-element.8, ...), kind=kLoop, calls=%fused_computation.64 | loop fusion | flops 48384 | bytes 91428 | tf_op jit(solution)/shard_map/gather | solution.py:111
  412.9 0.1 fusion.11
  413.0 29.5 %all-to-all-done.6 = bf16[16,672,128]{2,1,0:T(8,128)(2,1)S(1)} async-done(((bf16[16,672,128]{2,1,0:T(8,128)(2,1)}), bf16[16,672,128]{2,1,0:T(8,128)(2,1)S(1)}, u32[]{:S(2)}, u32[]{:S(2)}) %all-to-all-start.6) | async-done | bytes 2752544 | tf_op jit(solution)/shard_map/all_to_all | solution.py:103
  442.6 11.6 %gather_fusion.6 = bf16[5376,128]{1,0:T(8,128)(2,1)} fusion(bf16[10752,128]{1,0:T(8,128)(2,1)S(1)} %bitcast.80, s32[6144]{0:T(1024)S(1)} %pad_clamp_fusion.1), kind=kCustom, calls=%fused_computation.6 | custom fusion | bytes 2774016 | tf_op jit(solution)/shard_map/gather | solution.py:112
  454.2 3.7 reshape.191
  (17 shorter events, 0.2 us)
Async XLA Ops:
  0.6 2.3 copy-start
  23.4 8.2 %copy-start.2 = (f32[1,672,128]{2,1,0:T(8,128)S(1)}, f32[1,672,128]{2,1,0:T(8,128)}, u32[]{:S(2)}) copy-start(f32[1,672,128]{2,1,0:T(8,128)} %param.8) | copy-start | bytes 1032196
  52.0 6.7 %copy-start.3 = (f32[1,672,128]{2,1,0:T(8,128)S(1)}, f32[1,672,128]{2,1,0:T(8,128)}, u32[]{:S(2)}) copy-start(f32[1,672,128]{2,1,0:T(8,128)} %param.9) | copy-start | bytes 1032196
  251.6 5.9 %copy-start.6 = (s32[112]{0:T(128)S(1)}, s32[112]{0:T(128)}, u32[]{:S(2)}) copy-start(s32[112]{0:T(128)} %param.13) | copy-start | bytes 1348
  251.6 76.6 %all-to-all-start = ((f32[128,84,128]{2,1,0:T(8,128)}), f32[128,84,128]{2,1,0:T(8,128)}, u32[]{:S(2)}, u32[]{:S(2)}) async-start(f32[128,84,128]{2,1,0:T(8,128)} %get-tuple-element.40), calls=%async_computation | async-start | bytes 11534336 | tf_op jit(solution)/shard_map/all_to_all | solution.py:68
  328.2 9.4 %all-to-all-start.5 = ((f32[8,1,3,14,128]{4,1,3,2,0:T(1,128)}), f32[8,1,3,14,128]{4,1,3,2,0:T(1,128)S(1)}, u32[]{:S(2)}, u32[]{:S(2)}) async-start(f32[8,1,3,14,128]{4,1,3,2,0:T(1,128)} %copy.45), calls=%async_computation.5 | async-start | bytes 344064 | tf_op jit(solution)/shard_map/all_to_all | solution.py:83
  337.7 9.9 %all-to-all-start.3 = ((f32[8,1,3,14,128]{4,1,3,2,0:T(1,128)}), f32[8,1,3,14,128]{4,1,3,2,0:T(1,128)S(1)}, u32[]{:S(2)}, u32[]{:S(2)}) async-start(f32[8,1,3,14,128]{4,1,3,2,0:T(1,128)} %copy.43), calls=%async_computation.3 | async-start | bytes 344064 | tf_op jit(solution)/shard_map/all_to_all | solution.py:83
  344.8 35.3 %copy-start.4 = (f32[1,672,128]{2,1,0:T(8,128)S(1)}, f32[1,672,128]{2,1,0:T(8,128)}, u32[]{:S(2)}) copy-start(f32[1,672,128]{2,1,0:T(8,128)} %param.10) | copy-start | bytes 1032196
  357.0 15.7 %collective-permute-start.1 = (f32[3,336,128]{2,1,0:T(8,128)S(1)}, f32[3,336,128]{2,1,0:T(8,128)S(1)}, u32[]{:S(2)}, u32[]{:S(2)}) collective-permute-start(f32[3,336,128]{2,1,0:T(8,128)S(1)} %copy.46), channel_id=1, source_target_pairs={{16,0},{24,8},{32,16},{40,24},{48,32},{56,40},{64,48},{72,56},{80,... | collective-permute-start | bytes 1548296 | tf_op jit(solution)/shard_map/ppermute | solution.py:18
  358.3 14.7 %collective-permute-start = (f32[3,336,128]{2,1,0:T(8,128)S(1)}, f32[3,336,128]{2,1,0:T(8,128)S(1)}, u32[]{:S(2)}, u32[]{:S(2)}) collective-permute-start(f32[3,336,128]{2,1,0:T(8,128)S(1)} %copy.46), channel_id=1, source_target_pairs={{8,0},{16,8},{24,16},{32,24},{40,32},{48,40},{56,48},{64,56},{72,6... | collective-permute-start | bytes 1548296 | tf_op jit(solution)/shard_map/ppermute | solution.py:18
  380.1 21.2 %copy-start.5 = (s32[128,3]{0,1:T(4,128)S(1)}, s32[128,3]{0,1:T(4,128)}, u32[]{:S(2)}) copy-start(s32[128,3]{0,1:T(4,128)} %param.12) | copy-start | bytes 4612
  383.5 59.1 %all-to-all-start.6 = ((bf16[16,672,128]{2,1,0:T(8,128)(2,1)}), bf16[16,672,128]{2,1,0:T(8,128)(2,1)S(1)}, u32[]{:S(2)}, u32[]{:S(2)}) async-start(bf16[16,672,128]{2,1,0:T(8,128)(2,1)} %stack.5), calls=%async_computation.6 | async-start | bytes 5505024 | tf_op jit(solution)/shard_map/all_to_all | solution.py:103
  442.6 15.4 %copy-start.1 = (f32[1,672,128]{2,1,0:T(8,128)S(1)}, f32[1,672,128]{2,1,0:T(8,128)}, u32[]{:S(2)}) copy-start(f32[1,672,128]{2,1,0:T(8,128)} %param.7) | copy-start | bytes 1032196
